TPU v7x, 512 devices: a whole 4x8x8 slice. The times are simulated.
512 devices in a mesh: seq: 16 (over y, core), exp: 8 (over z), ffn: 4 (over x).
Axes of the slice: x: 4, y: 8, z: 8, core: 2. Of those that a mesh axis runs over, the one named last changes fastest.
Arguments:
- tokens: bfloat16 [4096, 2048], P('seq', 'ffn'), may hold values from -6 to 6
- out_grad: bfloat16 [4096, 2048], P('seq', 'ffn'), may hold values from -6 to 6
- gate_prob: bfloat16 [4096, 2], P('seq'), may hold values from 0.049804688 to 0.94921875
- routing: int32 [4096, 2], P('seq'), may hold values from 0 to 15, all different within a row; in each aligned block of 256 rows (0 to 255, 256 to 511, ...) at most 48 rows name the same one
- weight_in: bfloat16 [16, 2048, 8192], P('exp', 'ffn', 'seq'), may hold values from -0.125 to 0.125
- weight_out: bfloat16 [16, 8192, 2048], P('exp', 'seq', 'ffn'), may hold values from -0.0625 to 0.0625
Outputs:
- grad_tokens: bfloat16 [4096, 2048], P(('seq', 'exp'), 'ffn')
- grad_gate: float32 [4096, 2], P(('seq', 'exp'))
- grad_weight_in: bfloat16 [16, 2048, 8192], P('exp', 'ffn', 'seq')
- grad_weight_out: bfloat16 [16, 8192, 2048], P('exp', 'seq', 'ffn')
Inputs may be any that keep to these rules, and one draw needn't show every extreme that they name: `routing`: within the 256 rows of one token group no expert is named more than 48 times, and in every draw some expert is named exactly 48 times in some group; the 2 ids of a row differ, and every expert is named somewhere.
All inputs are finite; a program needn't handle non-finite values.
Results may differ from a plain program's by a relative error of at most 0.029.
Values may be sent and summed in bfloat16 or wider, within the bound.
A program may use at most 64 MiB of HBM per device.

v0:
```python
import jax
import jax.numpy as jnp
from jax import lax
from jax.sharding import PartitionSpec as P

gelu_scale = 0.7978845608028654
gelu_cubic = 0.044715


def gelu_parts(pre_act):
    inner_arg = gelu_scale * (pre_act + gelu_cubic * pre_act * pre_act * pre_act)
    tangent = jnp.tanh(inner_arg)
    activated = 0.5 * pre_act * (1.0 + tangent)
    slope_value = 0.5 * (1.0 + tangent) + 0.5 * pre_act * (1.0 - tangent * tangent) * gelu_scale * (
        1.0 + 3.0 * gelu_cubic * pre_act * pre_act
    )
    return (activated, slope_value)


def activate(hidden_sum, upper_sum, slot_gate):
    activated, slope_value = gelu_parts(hidden_sum)
    gate_column = slot_gate.astype(jnp.float32)[..., None]
    active = activated.astype(jnp.bfloat16)
    delta_rows = (gate_column * upper_sum * slope_value).astype(jnp.bfloat16)
    gate_term = jnp.sum(activated * upper_sum, axis=-1)
    return (active, delta_rows, gate_term)


def slot_selector(route_block, first_expert, expert_dev, capacity):
    blocks = route_block.shape[0]
    chosen_flat = route_block.reshape(blocks, -1) - first_expert
    local_ids = jnp.arange(expert_dev, dtype=jnp.int32)
    hit_table = (chosen_flat[:, :, None] == local_ids[None, None, :]).astype(jnp.int32)
    before = jnp.cumsum(hit_table, axis=1) - hit_table
    position = jnp.sum(hit_table * before, axis=2)
    is_local = jnp.sum(hit_table, axis=2)
    slot_row = chosen_flat * capacity + position
    row_ids = jnp.arange(expert_dev * capacity, dtype=jnp.int32)
    selector = (row_ids[None, :, None] == slot_row[:, None, :]) & (is_local[:, None, :] > 0)
    return selector.astype(jnp.bfloat16)


def arrange(picked, expert_dev):
    blocks = picked.shape[0]
    capacity = picked.shape[1] // expert_dev
    tail_shape = picked.shape[2:]
    grouped = picked.reshape((blocks, expert_dev, capacity) + tail_shape)
    grouped = jnp.swapaxes(grouped, 0, 1)
    return grouped.reshape((expert_dev, blocks * capacity) + tail_shape)


def gather_rows(selector, x_block, y_block, gate_block, expert_dev):
    blocks, row_total, assign = selector.shape
    tok_count = x_block.shape[1]
    by_token = selector.reshape(blocks, row_total, tok_count, assign // tok_count).sum(axis=3)
    x_pick = jnp.einsum(
        "brt,btd->brd", by_token, x_block, preferred_element_type=jnp.float32
    ).astype(jnp.bfloat16)
    y_pick = jnp.einsum(
        "brt,btd->brd", by_token, y_block, preferred_element_type=jnp.float32
    ).astype(jnp.bfloat16)
    gate_pick = jnp.einsum(
        "bra,ba->br",
        selector,
        gate_block.reshape(blocks, assign),
        preferred_element_type=jnp.float32,
    ).astype(jnp.bfloat16)
    return (
        arrange(x_pick, expert_dev),
        arrange(y_pick, expert_dev),
        arrange(gate_pick, expert_dev),
    )


def body(tokens, out_grad, gate_prob, routing, weight_in, weight_out):
    expert_dev = weight_in.shape[0]
    exp_count = lax.axis_size("exp")
    seq_count = lax.axis_size("seq")
    tok_count = tokens.shape[0]
    top_count = routing.shape[1]
    capacity = 3 * tok_count // (expert_dev * exp_count)
    first_expert = lax.axis_index("exp") * expert_dev
    own_selector = slot_selector(routing[None], first_expert, expert_dev, capacity)
    every_route = lax.all_gather(routing, "seq", axis=0, tiled=True)
    every_x, every_y, every_gate = (
        lax.all_gather(tokens, "seq", axis=0, tiled=True),
        lax.all_gather(out_grad, "seq", axis=0, tiled=True),
        lax.all_gather(gate_prob, "seq", axis=0, tiled=True),
    )
    every_selector = slot_selector(
        every_route.reshape(seq_count, tok_count, top_count), first_expert, expert_dev, capacity
    )
    slot_x, slot_y, slot_gate = gather_rows(
        every_selector,
        every_x.reshape(seq_count, tok_count, -1),
        every_y.reshape(seq_count, tok_count, -1),
        every_gate.reshape(seq_count, tok_count, top_count),
        expert_dev,
    )
    hidden_part = jnp.einsum("ecd,edf->ecf", slot_x, weight_in, preferred_element_type=jnp.float32)
    upper_part = jnp.einsum("ecd,efd->ecf", slot_y, weight_out, preferred_element_type=jnp.float32)
    hidden_sum, upper_sum = (
        lax.psum(hidden_part.astype(jnp.bfloat16), "ffn").astype(jnp.float32),
        lax.psum(upper_part.astype(jnp.bfloat16), "ffn").astype(jnp.float32),
    )
    active, delta_rows, gate_term = activate(hidden_sum, upper_sum, slot_gate)
    scaled = (slot_gate.astype(jnp.float32)[..., None] * slot_y.astype(jnp.float32)).astype(
        jnp.bfloat16
    )
    grad_weight_out = jnp.einsum(
        "ecf,ecd->efd", active, scaled, preferred_element_type=jnp.float32
    ).astype(jnp.bfloat16)
    grad_weight_in = jnp.einsum(
        "ecd,ecf->edf", slot_x, delta_rows, preferred_element_type=jnp.float32
    ).astype(jnp.bfloat16)
    back_rows = jnp.einsum(
        "ecf,edf->ecd", delta_rows, weight_in, preferred_element_type=jnp.float32
    )
    own_back, own_term = (
        lax.psum_scatter(
            back_rows.astype(jnp.bfloat16), "seq", scatter_dimension=1, tiled=True
        ).astype(jnp.float32),
        lax.psum_scatter(
            gate_term.astype(jnp.bfloat16), "seq", scatter_dimension=1, tiled=True
        ).astype(jnp.float32),
    )
    plain_selector = own_selector[0].astype(jnp.float32)
    row_total = plain_selector.shape[0]
    by_token = plain_selector.reshape(row_total, tok_count, top_count).sum(axis=2)
    flat_back = own_back.reshape(row_total, -1)
    token_back = jnp.einsum("rt,rd->td", by_token, flat_back, precision=lax.Precision.HIGHEST)
    gate_back = jnp.einsum(
        "r,ra->a", own_term.reshape(-1), plain_selector, precision=lax.Precision.HIGHEST
    ).reshape(tok_count, top_count)
    rows_part, gate_part = (
        lax.psum_scatter(
            token_back.astype(jnp.bfloat16), "exp", scatter_dimension=0, tiled=True
        ).astype(jnp.float32),
        lax.psum_scatter(
            gate_back.astype(jnp.bfloat16), "exp", scatter_dimension=0, tiled=True
        ).astype(jnp.float32),
    )
    return (rows_part.astype(jnp.bfloat16), gate_part, grad_weight_in, grad_weight_out)


def solution(mesh):
    return jax.shard_map(
        body,
        mesh=mesh,
        in_specs=(
            P("seq", "ffn"),
            P("seq", "ffn"),
            P("seq", None),
            P("seq", None),
            P("exp", "ffn", "seq"),
            P("exp", "seq", "ffn"),
        ),
        out_specs=(
            P(("seq", "exp"), "ffn"),
            P(("seq", "exp"), None),
            P("exp", "ffn", "seq"),
            P("exp", "seq", "ffn"),
        ),
        check_vma=False,
    )
```

profile of v0, /device:TPU:1, one launch (start us, length us, event | category | flops | bytes accessed | tf_op | source)
XLA Modules:
  0.0 412.2 jit_solution(10238209649646708991)
XLA Ops:
  8.7 21.2 %all_gather.12 = s32[4096,2]{0,1:T(2,128)S(1)} all-gather(s32[256,2]{0,1:T(2,128)} %param.9), channel_id=1, replica_groups=mesh['seq'=16,'exp'=8,'ffn'=4] {'seq'}, dimensions={0}, use_global_device_ids=true | all-gather | bytes 34816 | tf_op jit(solution)/shard_map/all_gather | solution.py:84
  30.6 1.2 sub.61
  31.9 1.2 sub.60
  33.1 2.3 reduce-window.16
  37.3 23.6 %all-gather.5.cloned.1.call-done = bf16[4096,512]{1,0:T(8,128)(2,1)} async-done(((bf16[256,512]{1,0:T(8,128)(2,1)}), bf16[4096,512]{1,0:T(8,128)(2,1)}) %all-gather.5.cloned.1.call-update) | async-done | bytes 4194320 | tf_op jit(solution)/shard_map/all_gather | solution.py:86
  60.9 3.0 convolution_convert_fusion.3
  64.0 42.1 %all-gather.3.cloned.1.call-done = bf16[4096,512]{1,0:T(8,128)(2,1)} async-done(((bf16[256,512]{1,0:T(8,128)(2,1)}), bf16[4096,512]{1,0:T(8,128)(2,1)}) %all-gather.3.cloned.1.call-update) | async-done | bytes 4194320 | tf_op jit(solution)/shard_map/all_gather | solution.py:87
  106.1 3.0 convolution_convert_fusion.4
  109.3 2.2 convolution_convert_fusion.1
  111.5 2.2 convolution_convert_fusion.2
  113.8 16.5 %all_gather.13 = bf16[4096,2]{0,1:T(2,128)(2,1)S(1)} all-gather(bf16[256,2]{0,1:T(2,128)(2,1)S(1)} %copy-done.7), channel_id=1, replica_groups=mesh['seq'=16,'exp'=8,'ffn'=4] {'seq'}, dimensions={0}, use_global_device_ids=true | all-gather | bytes 17408 | tf_op jit(solution)/shard_map/all_gather | solution.py:88
  130.8 1.7 reshape.336
  133.3 66.0 %all-reduce.3.cloned.1.call-done = (bf16[2,768,512]{2,1,0:T(8,128)(2,1)}, bf16[2,768,512]{2,1,0:T(8,128)(2,1)}) async-done(((bf16[2,768,512]{2,1,0:T(8,128)(2,1)}, bf16[2,768,512]{2,1,0:T(8,128)(2,1)}), (bf16[2,768,512]{2,1,0:T(8,128)(2,1)}, bf16[2,768,512]{2,1,0:T(8,128)(2,1)})) %all-reduce.3.cloned.1.call-update) | async-done | bytes 3145744 | tf_op jit(solution)/shard_map/psum | solution.py:103
  199.3 5.9 %fusion.7 = (bf16[2,768]{1,0:T(2,128)(2,1)S(1)}, bf16[2,768,512]{2,1,0:T(8,128)(2,1)}) fusion(bf16[2,768,512]{2,1,0:T(8,128)(2,1)} %get-tuple-element.9, bf16[2,768,512]{2,1,0:T(8,128)(2,1)} %get-tuple-element.8, f32[2,768]{1,0:T(2,128)S(1)} %reshape.329), kind=kLoop, calls=%fused_computation.16 | loop fusion | flops 19659264 | bytes 4727808 | tf_op jit(solution)/shard_map/reduce_sum | solution.py:25
  205.2 0.8 copy.125
  206.1 3.7 convolution_convert_fusion
  212.0 50.8 %reduce-scatter.13.cloned.1.call-done = bf16[48,2]{1,0:T(8,128)(2,1)} async-done(((bf16[768,2]{1,0:T(8,128)(2,1)}), bf16[48,2]{1,0:T(8,128)(2,1)}) %reduce-scatter.13.cloned.1.call-update) | async-done | bytes 208
  262.7 0.8 copy.126
  264.8 60.5 %reduce-scatter.9.cloned.1.call-done = bf16[2,48,512]{2,1,0:T(8,128)(2,1)} async-done(((bf16[2,768,512]{2,1,0:T(8,128)(2,1)}), bf16[2,48,512]{2,1,0:T(8,128)(2,1)}) %reduce-scatter.9.cloned.1.call-update) | async-done | bytes 98320 | tf_op jit(solution)/shard_map/reduce_scatter | solution.py:120
  325.3 2.0 convolution_convert_fusion.6
  327.4 3.6 convolution_convert_fusion.5
  331.0 2.8 fusion.27
  333.7 29.8 %reduce-scatter.15.cloned.1.call-done = bf16[32,2]{1,0:T(8,128)(2,1)} async-done(((bf16[256,2]{1,0:T(8,128)(2,1)}), bf16[32,2]{1,0:T(8,128)(2,1)}) %reduce-scatter.15.cloned.1.call-update) | async-done | bytes 144
  364.8 40.5 %reduce-scatter.11.cloned.1.call-done = bf16[32,512]{1,0:T(8,128)(2,1)} async-done(((bf16[256,512]{1,0:T(8,128)(2,1)}), bf16[32,512]{1,0:T(8,128)(2,1)}) %reduce-scatter.11.cloned.1.call-update) | async-done | bytes 32784 | tf_op jit(solution)/shard_map/reduce_scatter | solution.py:136
  (86 shorter events, 10.5 us)
Async XLA Ops:
  7.2 102.1 %copy-start = (bf16[2,512,512]{2,1,0:T(8,128)(2,1)S(1)}, bf16[2,512,512]{2,1,0:T(8,128)(2,1)}, u32[]{:S(2)}) copy-start(bf16[2,512,512]{2,1,0:T(8,128)(2,1)} %param.10) | copy-start | bytes 3145732
  7.2 53.7 %all-gather.5.cloned.1.call-start = ((), (), s32[]{:S(2)}) async-start(), calls=%async_computation.5 | async-start | bytes 4456448 | tf_op jit(solution)/shard_map/all_gather | solution.py:86
  7.9 98.2 %all-gather.3.cloned.1.call-start = ((), (), s32[]{:S(2)}) async-start(), calls=%async_computation.4 | async-start | bytes 4456448 | tf_op jit(solution)/shard_map/all_gather | solution.py:87
  8.7 190.6 %all-reduce.3.cloned.1.call-start = ((), (), s32[]{:S(2)}) async-start(), calls=%async_computation.10 | async-start | bytes 6291456 | tf_op jit(solution)/shard_map/psum | solution.py:103
  64.0 45.3 %copy-start.1 = (bf16[16,2,48,512]{3,2,0,1:T(8,128)(2,1)}, bf16[16,2,48,512]{3,2,0,1:T(8,128)(2,1)S(1)}, u32[]{:S(2)}) copy-start(bf16[16,2,48,512]{3,2,0,1:T(8,128)(2,1)S(1)} %copy.116) | copy-start | bytes 4718596
  109.1 2.3 copy-start.8
  109.3 2.2 copy-start.3
  111.5 2.3 copy-start.7
  113.7 149.0 %reduce-scatter.13.cloned.1.call-start = ((), (), s32[]{:S(2)}) async-start(), calls=%async_computation.8 | async-start | bytes 208896
  206.0 3.9 copy-start.6
  206.1 119.2 %reduce-scatter.9.cloned.1.call-start = ((), (), s32[]{:S(2)}) async-start(), calls=%async_computation.6 | async-start | bytes 1671168 | tf_op jit(solution)/shard_map/reduce_scatter | solution.py:120
  206.1 121.2 %copy-start.2 = (bf16[16,2,48,512]{3,2,0,1:T(8,128)(2,1)S(1)}, bf16[16,2,48,512]{3,2,0,1:T(8,128)(2,1)}, u32[]{:S(2)}) copy-start(bf16[16,2,48,512]{3,2,0,1:T(8,128)(2,1)} %copy-done.1) | copy-start | bytes 4718596
  209.8 153.6 %reduce-scatter.15.cloned.1.call-start = ((), (), s32[]{:S(2)}) async-start(), calls=%async_computation.9 | async-start | bytes 73728
  264.8 140.6 %reduce-scatter.11.cloned.1.call-start = ((), (), s32[]{:S(2)}) async-start(), calls=%async_computation.7 | async-start | bytes 294912 | tf_op jit(solution)/shard_map/reduce_scatter | solution.py:136
  327.4 3.6 copy-start.4
  327.4 3.6 copy-start.5
Sparse Core Ops, SparseCore 0:
  10.1 50.7 all-gather.4
  63.0 43.0 all-gather.2
  113.8 85.3 all-reduce.2
  206.2 56.4 reduce-scatter.12
  265.6 59.6 reduce-scatter.8
  328.0 35.4 reduce-scatter.14
  367.1 38.2 reduce-scatter.10
where the time goes:
time: 417 us; the launch traced here: 412 us
  waiting for transfers between devices  315 us (76%)
  blocking collectives  37.7 us (9%)
  matrix products  23.3 us (6%)
  between operations  14.4 us (3%)
  local copies, waits for them, and re-layouts  11.2 us (3%)
  other arithmetic  10.6 us (3%)
    unnamed x9, waiting for transfers between devices  82 us
    psum x1, waiting for transfers between devices, body(): lax.psum(hidden_part.astype(jnp.bfloat16), 'ffn').astype(jnp.float32)  66 us
    reduce_scatter x1, waiting for transfers between devices, body(): lax.psum_scatter(back_rows.astype(jnp.bfloat16), 'seq', scatter_dimension...  60.5 us
    all_gather x1, waiting for transfers between devices, body(): lax.all_gather(out_grad, 'seq', axis=0, tiled=True)  42.1 us
    reduce_scatter x1, waiting for transfers between devices, body(): lax.psum_scatter(token_back.astype(jnp.bfloat16), 'exp', scatter_dimensio...  40.5 us
    all_gather x1, waiting for transfers between devices, body(): lax.all_gather(tokens, 'seq', axis=0, tiled=True)  23.6 us
    all_gather x1, blocking collectives, body(): every_route = lax.all_gather(routing, 'seq', axis=0, tiled=True)  21.2 us
    all_gather x1, blocking collectives, body(): lax.all_gather(gate_prob, 'seq', axis=0, tiled=True)  16.5 us
  transfers between devices with their start and end apart: 7, of which 7 were waited for; matrix products, arithmetic and copies ran while one was open for 7% of the time, Pallas kernels for 0%

commit v1 on v0

v1 whole, which is shorter than its diff:
```python
import functools

import jax
import jax.numpy as jnp
from jax import lax
from jax.experimental import pallas as pl
from jax.experimental.pallas import tpu as pltpu
from jax.sharding import PartitionSpec as P

MESH = pl.DeviceIdType.MESH
BF16, F32 = jnp.bfloat16, jnp.float32
gelu_scale = 0.7978845608028654
gelu_cubic = 0.044715


def gelu_parts(pre_act):
    square = pre_act * pre_act
    tangent = jnp.tanh(gelu_scale * pre_act * (1.0 + gelu_cubic * square))
    half = 0.5 * (1.0 + tangent)
    slope = half + 0.5 * pre_act * (1.0 - tangent * tangent) * gelu_scale * (
        1.0 + 3.0 * gelu_cubic * square
    )
    return pre_act * half, slope


def dot(a, b, over):
    return lax.dot_general(a, b, ((over[:1], over[1:]), ((), ())), preferred_element_type=F32)


def split(value):
    high = value.astype(BF16)
    return high, (value - high.astype(F32)).astype(BF16)


def kernel(
    ny, nz, route, gate, tok_h, og_h, win_h, wout_h,
    gtok, ggate, gwi_h, gwo_h,
    tok, og, win, wout, xy, sel, part, r1, r2, s1, ad, bk, pb, ys, yr,
    g, gx, gs, gp, gt, gy, tb, zr, gz, gzr, gwi, gwo,
    in_sem, out_sem, ring_send, ring_recv, sib_send, sib_recv,
    r1_send, r1_recv, r2_send, r2_recv, a1_send, a1_recv, a2_send, a2_recv,
    pb_send, pb_recv, y_send, y_recv,
    gx_send, gx_recv, gp_send, gp_recv, gy_send, gy_recv, z_send, z_recv, gz_send, gz_recv,
):
    s, z, x = lax.axis_index("seq"), lax.axis_index("exp"), lax.axis_index("ffn")
    y, c = s // 2, s % 2
    sib = {"seq": s + 1 - 2 * c}
    xa, xb = {"ffn": x + 1 - 2 * (x % 2)}, {"ffn": 3 - x}
    h1, q1 = ((x + 1) // 2) % 2, x // 2
    h2, q2 = x // 2, x % 2
    units = 2 * ny
    cap = xy.shape[4]
    tokens = tok.shape[0]
    hid = win.shape[2]

    def along_y(step):
        return {"seq": ((y + step + ny) % ny) * 2 + c}

    def along_z(step):
        return {"exp": (z + step) % nz}

    def along_x(step):
        return {"ffn": (x + step) % 4}

    def send(src, dst, ssem, rsem, where):
        pltpu.make_async_remote_copy(
            src_ref=src, dst_ref=dst, send_sem=ssem, recv_sem=rsem,
            device_id=where, device_id_type=MESH,
        ).start()

    def done(ref, sem):
        pltpu.make_async_copy(ref, ref, sem).wait()

    loads = [
        pltpu.make_async_copy(a, b, in_sem.at[i])
        for i, (a, b) in enumerate(((tok_h, tok), (og_h, og), (win_h, win), (wout_h, wout)))
    ]
    for load in loads:
        load.start()

    barrier = pltpu.get_barrier_semaphore()
    peers = [sib]
    peers += [along_y(d) for d in range(1, ny)]
    peers += [along_x(d) for d in range(1, 4)]
    peers += [along_z(d) for d in range(1, nz)]
    for peer in peers:
        pl.semaphore_signal(barrier, inc=1, device_id=peer, device_id_type=MESH)

    ids = [route[k : k + 1, :] for k in range(2)]
    probs = [gate[k : k + 1, :].astype(F32) for k in range(2)]
    named = [[r == 2 * z + e for r in ids] for e in range(2)]
    taken = [jnp.where(named[e][0] | named[e][1], 1.0, 0.0) for e in range(2)]
    weight = [
        jnp.where(named[e][0], probs[0], jnp.where(named[e][1], probs[1], 1.0)) for e in range(2)
    ]
    row_at = lax.broadcasted_iota(jnp.int32, (tokens, tokens), 0)
    col_at = lax.broadcasted_iota(jnp.int32, (tokens, tokens), 1)
    earlier = jnp.where(row_at < col_at, 1.0, 0.0).astype(BF16)
    slot_at = lax.broadcasted_iota(jnp.int32, (cap, tokens), 0).astype(F32)
    g[...] = jnp.zeros_like(g)
    loads[0].wait()
    loads[1].wait()
    for e in range(2):
        before = dot(jnp.broadcast_to(taken[e], (16, tokens)).astype(BF16), earlier, (1, 0))
        hit = (before[0:1, :] == slot_at) & (taken[e] > 0.5)
        sel[e] = jnp.where(hit, 1.0, 0.0).astype(BF16)
        scaled_sel = jnp.where(hit, weight[e], 0.0).astype(BF16)
        xy[0, e, 0, c] = dot(sel[e], tok[...], (1, 0)).astype(BF16)
        xy[1, e, 0, c] = dot(scaled_sel, og[...], (1, 0)).astype(BF16)
        if e == 0:
            pl.semaphore_wait(barrier, len(peers))
        reach = (ny // 2, ny // 2 - 1) if e == 0 else (ny // 2 - 1, ny // 2)
        own = xy.at[:, e, 0, c]
        send(own, own, sib_send, sib_recv.at[e, 0], sib)
        if reach[0] > 0:
            send(own, xy.at[:, e, 1, c], ring_send, ring_recv.at[e, 1], along_y(-1))
        if reach[1] > 0:
            send(own, xy.at[:, e, ny - 1, c], ring_send, ring_recv.at[e, ny - 1], along_y(1))
    loads[2].wait()
    loads[3].wait()

    def far(i):
        odd = i % 2
        return odd * ((i + 1) // 2) + (1 - odd) * ((ny - i // 2) % ny)

    def unit(u):
        e = u // ny
        i = u - e * ny
        return e, far(i + e * (ny - 1 - 2 * i))

    def pass_on(e, j):
        reach = (ny // 2, ny // 2 - 1) if e == 0 else (ny // 2 - 1, ny // 2)
        here = xy.at[:, e, j, c]
        done(here, ring_recv.at[e, j])
        send(here, here, sib_send, sib_recv.at[e, j], sib)

        @pl.when((j <= reach[0]) & (j < reach[0]))
        def _():
            send(here, xy.at[:, e, j + 1, c], ring_send, ring_recv.at[e, j + 1], along_y(-1))

        @pl.when((j >= ny - reach[1]) & (j > ny - reach[1]))
        def _():
            send(here, xy.at[:, e, j - 1, c], ring_send, ring_recv.at[e, j - 1], along_y(1))

    def products(u):
        e, j = unit(u)
        done(xy.at[:, e, j, 0], sib_recv.at[e, j])
        values = (
            dot(xy[0, e, j].reshape(2 * cap, -1), win[e], (1, 0)).astype(BF16),
            dot(xy[1, e, j].reshape(2 * cap, -1), wout[e], (1, 1)).astype(BF16),
        )
        for half in range(2):
            for b in range(4):
                for a in range(2):
                    part[u, half, b, a] = values[a][
                        half * cap : (half + 1) * cap, b * 128 : (b + 1) * 128
                    ]
        send(part.at[u, 0, pl.ds(2 * (1 - h1), 2)], r1.at[u, 0], r1_send, r1_recv.at[u], xa)
        send(part.at[u, 1, pl.ds(2 * (1 - h2), 2)], r1.at[u, 1], r1_send, r1_recv.at[u], xb)

    def halve(u):
        done(r1.at[u], r1_recv.at[u])
        for half, (h, q, to) in enumerate(((h1, q1, xb), (h2, q2, xa))):
            s1[u, half] = (
                part[u, half, 2 * h + 1 - q].astype(F32) + r1[u, half, 1 - q].astype(F32)
            ).astype(BF16)
            send(s1.at[u, half], r2.at[u, half], r2_send, r2_recv.at[u], to)

    def activate(u):
        e, j = unit(u)
        done(r2.at[u], r2_recv.at[u])
        terms = []
        for half, (h, q, to) in enumerate(((h1, q1, xb), (h2, q2, xa))):
            total = (
                part[u, half, 2 * h + q].astype(F32)
                + r1[u, half, q].astype(F32)
                + r2[u, half].astype(F32)
            )
            activated, slope = gelu_parts(total[0])
            ad[e, 2 * h + q, 0, j, half] = activated.astype(BF16)
            ad[e, 2 * h + q, 1, j, half] = (total[1] * slope).astype(BF16)
            piece = ad.at[e, 2 * h + q, :, j, half]
            send(piece, piece, a1_send, a1_recv.at[u], to)
            terms.append(activated * total[1])
        high, low = split(jnp.concatenate(terms, axis=0))
        ones = jnp.ones((16, 2 * 128), BF16)
        summed = dot(ones, jnp.concatenate((high, low), axis=1), (1, 1))
        g[pl.ds(8 * j + e, 1), 0 : 2 * cap] = summed[0:1, :]

    def widen(u):
        e, j = unit(u)
        done(r2.at[u], a1_recv.at[u])
        for half, (h, to) in enumerate(((h1, xa), (h2, xb))):
            piece = ad.at[e, pl.ds(2 * h, 2), :, j, half]
            send(piece, piece, a2_send, a2_recv.at[u], to)

    def back(u):
        e, j = unit(u)
        done(r1.at[u], a2_recv.at[u])
        delta = jnp.concatenate(
            [ad[e, b, 1, j].reshape(2 * cap, 128) for b in range(4)], axis=1
        )
        bk[u] = dot(delta, win[e], (1, 1)).astype(BF16).reshape(2, cap, -1)
        send(bk.at[u, 1 - c], pb.at[u], pb_send, pb_recv.at[u], sib)

    def deliver(u):
        e, j = unit(u)
        done(pb.at[u], pb_recv.at[u])
        both = (bk[u, c].astype(F32) + pb[u].astype(F32)).astype(BF16)

        @pl.when(j == 0)
        def _():
            yr[e, 0] = both

        @pl.when(j > 0)
        def _():
            ys[u] = both
            send(ys.at[u], yr.at[e, j], y_send, y_recv.at[e, j], along_y(j))

    def weight_grads(e, p):
        rows = 2 * ny * cap
        cols = pl.ds(p * (hid // 2), hid // 2)
        act, delta = (
            jnp.concatenate([ad[e, 2 * p + b, a].reshape(rows, 128) for b in range(2)], axis=1)
            for a in range(2)
        )
        gwi[e, :, cols] = dot(xy[0, e].reshape(rows, -1), delta, (0, 0)).astype(BF16)
        gwo[e, cols, :] = dot(act, xy[1, e].reshape(rows, -1), (0, 0)).astype(BF16)

    def store_grads(e):
        return [
            pltpu.make_async_copy(gwi.at[e], gwi_h.at[e], out_sem.at[e, 0]),
            pltpu.make_async_copy(gwo.at[e], gwo_h.at[e], out_sem.at[e, 1]),
        ]

    def step(k, carry):
        def stage(lag, work):
            @pl.when((k >= lag) & (k < units + lag))
            def _():
                work(k - lag)

        stage(1, halve)
        stage(2, activate)
        stage(3, widen)
        stage(0, products)

        @pl.when(k < ny - 1)
        def _():
            pass_on(0, far(k + 1))

        @pl.when((k > 0) & (k < ny))
        def _():
            pass_on(1, far(k))

        stage(4, back)
        stage(5, deliver)

        @pl.when(k == units + 1)
        def _():
            for d in range(1, 4):
                send(g, gx.at[d - 1], gx_send, gx_recv, along_x(d))

        @pl.when(k == units + 2)
        def _():
            done(gx, gx_recv)
            gs[...] = g[...] + gx[0] + gx[1] + gx[2]
            send(gs, gp, gp_send, gp_recv, sib)

        @pl.when(k == units + 3)
        def _():
            done(gp, gp_recv)
            gt[...] = (gs[...] + gp[...]).reshape(gt.shape)
            gy[0] = gt[0]
            for d in range(1, ny):
                send(gt.at[d], gy.at[d], gy_send, gy_recv, along_y(d))

        for p in range(2):
            @pl.when(k == ny + 4 + p)
            def _():
                weight_grads(0, p)

        @pl.when(k == ny + 6)
        def _():
            for copy in store_grads(0):
                copy.start()

        return carry

    lax.fori_loop(0, units + 5, step, 0)

    rows = []
    for e in range(2):
        for j in range(1, ny):
            done(yr.at[e, j], y_recv.at[e, j])
        rows.append(jnp.sum(yr[e].astype(F32), axis=0).astype(BF16))
    for e in range(2):
        own = dot(sel[e], rows[e], (0, 0))
        total = own if e == 0 else total + own
    tb[...] = total.astype(BF16).reshape(tb.shape)
    for d in range(1, nz):
        send(tb.at[(z + d) % nz], zr.at[d], z_send, z_recv, along_z(d))

    done(gy.at[pl.ds(1, ny - 1)], gy_recv)
    term = jnp.sum(gy[...], axis=0)
    term = jnp.where(c == 0, term[:, 0:cap], term[:, cap : 2 * cap])
    term = jnp.concatenate((term, jnp.zeros_like(term)), axis=0)
    high, low = split(term)
    at_token = []
    for e in range(2):
        value = dot(high, sel[e], (1, 0)) + dot(low, sel[e], (1, 0))
        at_token.append(value[e : e + 1, :] / weight[e])
    gz[...] = jnp.zeros_like(gz)
    for k in range(2):
        gz[k : k + 1, :] = jnp.where(named[0][k], at_token[0], 0.0) + jnp.where(
            named[1][k], at_token[1], 0.0
        )
    for d in range(1, nz):
        send(gz, gzr.at[d], gz_send, gz_recv, along_z(d))

    for p in range(2):
        weight_grads(1, p)
    for copy in store_grads(1):
        copy.start()

    out = tb[z].astype(F32)
    gates = gz[...]
    if nz > 1:
        done(zr.at[pl.ds(1, nz - 1)], z_recv)
        done(gzr.at[pl.ds(1, nz - 1)], gz_recv)
        for d in range(1, nz):
            out = out + zr[d].astype(F32)
            gates = gates + gzr[d]
    gtok[...] = out.astype(BF16)
    mine = gtok.shape[0]
    pick = jnp.where(
        lax.broadcasted_iota(jnp.int32, (mine, tokens), 1)
        == lax.broadcasted_iota(jnp.int32, (mine, tokens), 0) + z * mine,
        1.0,
        0.0,
    ).astype(BF16)
    high, low = split(jnp.concatenate((gates, jnp.zeros_like(gates)), axis=0))
    ggate[...] = (dot(pick, high, (1, 1)) + dot(pick, low, (1, 1)))[:, 0:2]

    done(xy.at[:, :, pl.ds(0, ny - 1), 0], ring_send)
    done(xy.at[:, :, :, 0], sib_send)
    done(r1, r1_send)
    done(r2, r2_send)
    done(r2, a1_send)
    done(r1, a2_send)
    done(pb, pb_send)
    done(ys.at[pl.ds(0, 2 * (ny - 1))], y_send)
    done(gx, gx_send)
    done(gp, gp_send)
    done(gy.at[pl.ds(1, ny - 1)], gy_send)
    if nz > 1:
        done(zr.at[pl.ds(1, nz - 1)], z_send)
        done(gzr.at[pl.ds(1, nz - 1)], gz_send)
    for e in range(2):
        for copy in store_grads(e):
            copy.wait()


def body(ny, nz, tokens, out_grad, gate_prob, routing, weight_in, weight_out):
    tok, width = tokens.shape
    hid = weight_in.shape[2]
    cap = 3 * tok // (2 * nz)
    units = 2 * ny
    mine = tok // nz
    vmem, anywhere = (pl.BlockSpec(memory_space=m) for m in (pltpu.VMEM, pl.ANY))
    buf = pltpu.VMEM
    dma = pltpu.SemaphoreType.DMA
    return pl.pallas_call(
        functools.partial(kernel, ny, nz),
        out_shape=(
            jax.ShapeDtypeStruct((mine, width), BF16),
            jax.ShapeDtypeStruct((mine, 2), F32),
            jax.ShapeDtypeStruct(weight_in.shape, BF16),
            jax.ShapeDtypeStruct(weight_out.shape, BF16),
        ),
        in_specs=[vmem, vmem] + [anywhere] * 4,
        out_specs=(vmem, vmem, anywhere, anywhere),
        scratch_shapes=[
            buf((tok, width), BF16),
            buf((tok, width), BF16),
            buf(weight_in.shape, BF16),
            buf(weight_out.shape, BF16),
            buf((2, 2, ny, 2, cap, width), BF16),
            buf((2, cap, tok), BF16),
            buf((units, 2, 4, 2, cap, 128), BF16),
            buf((units, 2, 2, 2, cap, 128), BF16),
            buf((units, 2, 2, cap, 128), BF16),
            buf((units, 2, 2, cap, 128), BF16),
            buf((2, 4, 2, ny, 2, cap, 128), BF16),
            buf((units, 2, cap, width), BF16),
            buf((units, cap, width), BF16),
            buf((units, cap, width), BF16),
            buf((2, ny, cap, width), BF16),
            buf((8 * ny, 128), F32),
            buf((3, 8 * ny, 128), F32),
            buf((8 * ny, 128), F32),
            buf((8 * ny, 128), F32),
            buf((ny, 8, 128), F32),
            buf((ny, 8, 128), F32),
            buf((nz, mine, width), BF16),
            buf((nz, mine, width), BF16),
            buf((8, tok), F32),
            buf((nz, 8, tok), F32),
            buf(weight_in.shape, BF16),
            buf(weight_out.shape, BF16),
            dma((4,)),
            dma((2, 2)),
            dma,
            dma((2, ny)),
            dma,
            dma((2, ny)),
            dma,
            dma((units,)),
            dma,
            dma((units,)),
            dma,
            dma((units,)),
            dma,
            dma((units,)),
            dma,
            dma((units,)),
            dma,
            dma((2, ny)),
            dma,
            dma,
            dma,
            dma,
            dma,
            dma,
            dma,
            dma,
            dma,
            dma,
        ],
        compiler_params=pltpu.CompilerParams(
            collective_id=0, has_side_effects=True, vmem_limit_bytes=48 * 2**20
        ),
        name="expert_backward",
    )(routing.T, gate_prob.T, tokens, out_grad, weight_in, weight_out)


def solution(mesh):
    ny, nz = mesh.shape["seq"] // 2, mesh.shape["exp"]
    return jax.shard_map(
        functools.partial(body, ny, nz),
        mesh=mesh,
        in_specs=(
            P("seq", "ffn"),
            P("seq", "ffn"),
            P("seq", None),
            P("seq", None),
            P("exp", "ffn", "seq"),
            P("exp", "seq", "ffn"),
        ),
        out_specs=(
            P(("seq", "exp"), "ffn"),
            P(("seq", "exp"), None),
            P("exp", "ffn", "seq"),
            P("exp", "seq", "ffn"),
        ),
        check_vma=False,
    )
```

time: 417 us -> 132 us (0.32)
  waiting for transfers between devices: 315 us -> 0 us
  Pallas kernels: 0 us -> 122 us
  blocking collectives: 37.7 us -> 0 us
  matrix products: 23.3 us -> 0 us
  between operations: 14.4 us -> 0.66 us
  other arithmetic: 10.6 us -> 0 us
    pallas_call x0 -> x1, Pallas kernels: none -> 122 us  [body(): pl.pallas_call(functools.partial(kernel, ny, nz), out_shape=(jax.ShapeDty...]
    reduce_scatter x2 -> x0, waiting for transfers between devices: 101 us -> none  [the longest x1 60.5 us: body(): lax.psum_scatter(back_rows.astype(jnp.bfloat16), 'seq', scatter_dimension...]
    unnamed x9 -> x0, waiting for transfers between devices: 82 us -> none
    psum x1 -> x0, waiting for transfers between devices: 66 us -> none  [body(): lax.psum(hidden_part.astype(jnp.bfloat16), 'ffn').astype(jnp.float32)]
    all_gather x2 -> x0, waiting for transfers between devices: 65.7 us -> none  [the longest x1 42.1 us: body(): lax.all_gather(out_grad, 'seq', axis=0, tiled=True)]
    all_gather x2 -> x0, blocking collectives: 37.7 us -> none  [the longest x1 21.2 us: body(): every_route = lax.all_gather(routing, 'seq', axis=0, tiled=True)]
    dot_general x10 -> x0, matrix products: 23.3 us -> none  [the longest x1 3.69 us: body(): jnp.einsum('ecf,edf->ecd', delta_rows, weight_in, preferred_element_type=...]
    reduce_sum x5 -> x0, other arithmetic: 6.82 us -> none  [the longest x1 5.93 us: activate(): gate_term = jnp.sum(activated * upper_sum, axis=-1)]
  transfers between devices with their start and end apart: 7 -> 0, of which waited for: 7 -> 0; matrix products, arithmetic and copies ran while one was open for 7% -> 0% of each run, Pallas kernels for 0% -> 0%
where the time goes in v1:
time: 132 us; the launch traced here: 131 us
  Pallas kernels  122 us (92%)
  local copies, waits for them, and re-layouts  8.22 us (6%)
    pallas_call x1, Pallas kernels, body(): pl.pallas_call(functools.partial(kernel, ny, nz), out_shape=(jax.ShapeDty...  122 us
    unnamed x15, local copies, waits for them, and re-layouts  7.58 us

profile of v1, /device:TPU:1, one launch (start us, length us, event | category | flops | bytes accessed | tf_op | source)
XLA Modules:
  0.0 131.3 jit_solution(14677877868551950203)
XLA Ops:
  0.6 0.0 copy-start.4
  0.6 0.0 copy-start.5
  0.7 0.7 copy-done.4
  1.3 0.0 copy-done.5
  1.3 0.0 copy-start
  1.3 1.2 copy-done
  2.6 0.0 copy-start.1
  2.6 1.2 copy-done.1
  3.8 0.0 copy-start.2
  3.8 0.9 copy-done.2
  4.7 0.0 copy-start.3
  4.7 0.9 copy-done.3
  5.7 122.4 %expert_backward.1 = (bf16[32,512]{1,0:T(8,128)(2,1)S(1)}, f32[32,2]{1,0:T(8,128)S(1)}, bf16[2,512,512]{2,1,0:T(8,128)(2,1)S(1)}, bf16[2,512,512]{2,1,0:T(8,128)(2,1)S(1)}) custom-call(s32[2,256]{1,0:T(2,128)S(1)} %bitcast.2, bf16[2,256]{1,0:T(2,128)(2,1)S(1)} %bitcast.3, bf16[256,512]{1,0:T(8,128)(2,1)S(1)} %copy-done.2, bf16[256,512]{1,0:T(8,128)(2,1)S(1)} %copy-done.3, ...), custom_call_target="tpu_custom_call" | custom-call | tf_op jit(solution)/shard_map/expert_backward/pallas_call | solution.py:372
  128.1 0.6 copy.10
  128.8 0.6 copy.14
  129.4 1.0 copy.15
  130.4 1.0 copy.16
Async XLA Ops:
  0.6 0.7 copy-start.4
  0.6 0.7 copy-start.5
  1.3 1.2 copy-start
  2.6 1.2 copy-start.1
  3.8 0.9 copy-start.2
  4.7 0.9 copy-start.3

commit v2 on v1

--- a/solution.py
+++ b/solution.py
@@ -11,6 +11,9 @@
 BF16, F32 = jnp.bfloat16, jnp.float32
 gelu_scale = 0.7978845608028654
 gelu_cubic = 0.044715
+VMEM_BYTES = 62 * 2**20
+LAGS = (2, 4, 6, 8, 9)
+SECOND = 5
 
 
 def gelu_parts(pre_act):
@@ -85,6 +88,15 @@
     peers += [along_z(d) for d in range(1, nz)]
     for peer in peers:
         pl.semaphore_signal(barrier, inc=1, device_id=peer, device_id_type=MESH)
+
+    def spread(e):
+        reach = (ny // 2, ny // 2 - 1) if e == 0 else (ny // 2 - 1, ny // 2)
+        own = xy.at[:, e, 0, c]
+        send(own, own, sib_send, sib_recv.at[e, 0], sib)
+        if reach[0] > 0:
+            send(own, xy.at[:, e, 1, c], ring_send, ring_recv.at[e, 1], along_y(-1))
+        if reach[1] > 0:
+            send(own, xy.at[:, e, ny - 1, c], ring_send, ring_recv.at[e, ny - 1], along_y(1))
 
     ids = [route[k : k + 1, :] for k in range(2)]
     probs = [gate[k : k + 1, :].astype(F32) for k in range(2)]
@@ -109,13 +121,8 @@
         xy[1, e, 0, c] = dot(scaled_sel, og[...], (1, 0)).astype(BF16)
         if e == 0:
             pl.semaphore_wait(barrier, len(peers))
-        reach = (ny // 2, ny // 2 - 1) if e == 0 else (ny // 2 - 1, ny // 2)
-        own = xy.at[:, e, 0, c]
-        send(own, own, sib_send, sib_recv.at[e, 0], sib)
-        if reach[0] > 0:
-            send(own, xy.at[:, e, 1, c], ring_send, ring_recv.at[e, 1], along_y(-1))
-        if reach[1] > 0:
-            send(own, xy.at[:, e, ny - 1, c], ring_send, ring_recv.at[e, ny - 1], along_y(1))
+        if e == 0:
+            spread(0)
     loads[2].wait()
     loads[3].wait()
 
@@ -126,7 +133,7 @@
     def unit(u):
         e = u // ny
         i = u - e * ny
-        return e, far(i + e * (ny - 1 - 2 * i))
+        return e, far((i + e) % ny)
 
     def pass_on(e, j):
         reach = (ny // 2, ny // 2 - 1) if e == 0 else (ny // 2 - 1, ny // 2)
@@ -239,34 +246,38 @@
             def _():
                 work(k - lag)
 
-        stage(1, halve)
-        stage(2, activate)
-        stage(3, widen)
+        stage(LAGS[0], halve)
+        stage(LAGS[1], activate)
+        stage(LAGS[2], widen)
         stage(0, products)
 
         @pl.when(k < ny - 1)
         def _():
             pass_on(0, far(k + 1))
 
-        @pl.when((k > 0) & (k < ny))
-        def _():
-            pass_on(1, far(k))
-
-        stage(4, back)
-        stage(5, deliver)
-
-        @pl.when(k == units + 1)
+        @pl.when(k == SECOND)
+        def _():
+            spread(1)
+
+        @pl.when((k > SECOND) & (k < SECOND + ny))
+        def _():
+            pass_on(1, far(k - SECOND))
+
+        stage(LAGS[3], back)
+        stage(LAGS[4], deliver)
+
+        @pl.when(k == units - 1 + LAGS[1])
         def _():
             for d in range(1, 4):
                 send(g, gx.at[d - 1], gx_send, gx_recv, along_x(d))
 
-        @pl.when(k == units + 2)
+        @pl.when(k == units - 1 + LAGS[2])
         def _():
             done(gx, gx_recv)
             gs[...] = g[...] + gx[0] + gx[1] + gx[2]
             send(gs, gp, gp_send, gp_recv, sib)
 
-        @pl.when(k == units + 3)
+        @pl.when(k == units - 1 + LAGS[3])
         def _():
             done(gp, gp_recv)
             gt[...] = (gs[...] + gp[...]).reshape(gt.shape)
@@ -275,18 +286,18 @@
                 send(gt.at[d], gy.at[d], gy_send, gy_recv, along_y(d))
 
         for p in range(2):
-            @pl.when(k == ny + 4 + p)
+            @pl.when(k == ny + LAGS[3] + p)
             def _():
                 weight_grads(0, p)
 
-        @pl.when(k == ny + 6)
+        @pl.when(k == ny + LAGS[3] + 2)
         def _():
             for copy in store_grads(0):
                 copy.start()
 
         return carry
 
-    lax.fori_loop(0, units + 5, step, 0)
+    lax.fori_loop(0, units + LAGS[4], step, 0)
 
     rows = []
     for e in range(2):
@@ -339,7 +350,7 @@
         0.0,
     ).astype(BF16)
     high, low = split(jnp.concatenate((gates, jnp.zeros_like(gates)), axis=0))
-    ggate[...] = (dot(pick, high, (1, 1)) + dot(pick, low, (1, 1)))[:, 0:2]
+    ggate[...] = (dot(high, pick, (1, 1)) + dot(low, pick, (1, 1)))[0:2, :]
 
     done(xy.at[:, :, pl.ds(0, ny - 1), 0], ring_send)
     done(xy.at[:, :, :, 0], sib_send)
@@ -360,6 +371,19 @@
             copy.wait()
 
 
+def hand_over(*refs):
+    given, out, held, sems = refs[:4], refs[4:8], refs[8:12], refs[12]
+    loads = [pltpu.make_async_copy(given[i], held[i], sems.at[0, i]) for i in range(4)]
+    stores = [pltpu.make_async_copy(held[i], out[i], sems.at[1, i]) for i in range(4)]
+    for load in loads:
+        load.start()
+    for load, store in zip(loads, stores):
+        load.wait()
+        store.start()
+    for store in stores:
+        store.wait()
+
+
 def body(ny, nz, tokens, out_grad, gate_prob, routing, weight_in, weight_out):
     tok, width = tokens.shape
     hid = weight_in.shape[2]
@@ -369,11 +393,11 @@
     vmem, anywhere = (pl.BlockSpec(memory_space=m) for m in (pltpu.VMEM, pl.ANY))
     buf = pltpu.VMEM
     dma = pltpu.SemaphoreType.DMA
-    return pl.pallas_call(
+    results = pl.pallas_call(
         functools.partial(kernel, ny, nz),
         out_shape=(
             jax.ShapeDtypeStruct((mine, width), BF16),
-            jax.ShapeDtypeStruct((mine, 2), F32),
+            jax.ShapeDtypeStruct((2, mine), F32),
             jax.ShapeDtypeStruct(weight_in.shape, BF16),
             jax.ShapeDtypeStruct(weight_out.shape, BF16),
         ),
@@ -437,10 +461,20 @@
             dma,
         ],
         compiler_params=pltpu.CompilerParams(
-            collective_id=0, has_side_effects=True, vmem_limit_bytes=48 * 2**20
+            collective_id=0, has_side_effects=True, vmem_limit_bytes=VMEM_BYTES
         ),
         name="expert_backward",
     )(routing.T, gate_prob.T, tokens, out_grad, weight_in, weight_out)
+    gtok, ggate, gwi, gwo = pl.pallas_call(
+        hand_over,
+        out_shape=tuple(jax.ShapeDtypeStruct(r.shape, r.dtype) for r in results),
+        in_specs=[anywhere] * 4,
+        out_specs=(anywhere,) * 4,
+        scratch_shapes=[buf(r.shape, r.dtype) for r in results] + [dma((2, 4))],
+        compiler_params=pltpu.CompilerParams(vmem_limit_bytes=VMEM_BYTES),
+        name="hand_over",
+    )(*results)
+    return gtok, ggate.T, gwi, gwo
 
 
 def solution(mesh):

time: 132 us -> 98.3 us (0.74)
  Pallas kernels: 122 us -> 97.1 us
  local copies, waits for them, and re-layouts: 8.22 us -> 0 us
    pallas_call x1, Pallas kernels: 122 us -> 94.5 us  [body(): pl.pallas_call(functools.partial(kernel, ny, nz), out_shape=(jax.ShapeDty...]
    unnamed x15 -> x0, local copies, waits for them, and re-layouts: 7.58 us -> none
    pallas_call x0 -> x1, Pallas kernels: none -> 2.63 us  [body(): pl.pallas_call(hand_over, out_shape=tuple((jax.ShapeDtypeStruct(r.shape,...]
where the time goes in v2:
time: 98.3 us; the launch traced here: 97.7 us
  Pallas kernels  97.1 us (99%)
    pallas_call x1, Pallas kernels, body(): pl.pallas_call(functools.partial(kernel, ny, nz), out_shape=(jax.ShapeDty...  94.5 us
    pallas_call x1, Pallas kernels, body(): pl.pallas_call(hand_over, out_shape=tuple((jax.ShapeDtypeStruct(r.shape,...  2.63 us

profile of v2, /device:TPU:1, one launch (start us, length us, event | category | flops | bytes accessed | tf_op | source)
XLA Modules:
  0.0 97.7 jit_solution(10277581992177859440)
XLA Ops:
  0.6 94.5 %expert_backward.1 = (bf16[32,512]{1,0:T(8,128)(2,1)}, f32[2,32]{1,0:T(2,128)}, bf16[2,512,512]{2,1,0:T(8,128)(2,1)}, bf16[2,512,512]{2,1,0:T(8,128)(2,1)}) custom-call(s32[2,256]{1,0:T(2,128)} %bitcast.3, bf16[2,256]{1,0:T(2,128)(2,1)} %bitcast.4, bf16[256,512]{1,0:T(8,128)(2,1)} %tok_h.1, bf16[256,512]{1,0:T(8,128)(2,1)} %og_h.1, ...), custom_call_target="tpu_custom_call" | custom-call | tf_op jit(solution)/shard_map/expert_backward/pallas_call | solution.py:396
  95.1 2.6 %hand_over.1 = (bf16[32,512]{1,0:T(8,128)(2,1)}, f32[2,32]{1,0:T(2,128)}, bf16[2,512,512]{2,1,0:T(8,128)(2,1)}, bf16[2,512,512]{2,1,0:T(8,128)(2,1)}) custom-call(bf16[32,512]{1,0:T(8,128)(2,1)} %get-tuple-element.12.refs_0_, f32[2,32]{1,0:T(2,128)} %get-tuple-element.13.refs_1_, bf16[2,512,512]{2,1,0:T(8,128)(2,1)} %get-tuple-element.14.refs_2_, ...), custom_call_target="tpu_custom_call" | custom-call | tf_op jit(solution)/shard_map/hand_over/pallas_call | solution.py:468

commit v3 on v2

--- a/solution.py
+++ b/solution.py
@@ -13,7 +13,7 @@
 gelu_cubic = 0.044715
 VMEM_BYTES = 62 * 2**20
 LAGS = (2, 4, 6, 8, 9)
-SECOND = 5
+SECOND = 1
 
 
 def gelu_parts(pre_act):
@@ -38,10 +38,11 @@
 def kernel(
     ny, nz, route, gate, tok_h, og_h, win_h, wout_h,
     gtok, ggate, gwi_h, gwo_h,
-    tok, og, win, wout, xy, sel, part, r1, r2, s1, ad, bk, pb, ys, yr,
+    tok, og, win, wout, xy, sel, part, r1, r2, s1, act, dlt, bk, pb, ys, yr,
     g, gx, gs, gp, gt, gy, tb, zr, gz, gzr, gwi, gwo,
     in_sem, out_sem, ring_send, ring_recv, sib_send, sib_recv,
-    r1_send, r1_recv, r2_send, r2_recv, a1_send, a1_recv, a2_send, a2_recv,
+    r1_send, r1_recv, r2_send, r2_recv, d1_send, d1_recv, d2_send, d2_recv,
+    a1_send, a1_recv, a2_send, a2_recv,
     pb_send, pb_recv, y_send, y_recv,
     gx_send, gx_recv, gp_send, gp_recv, gy_send, gy_recv, z_send, z_recv, gz_send, gz_recv,
 ):
@@ -92,7 +93,6 @@
     def spread(e):
         reach = (ny // 2, ny // 2 - 1) if e == 0 else (ny // 2 - 1, ny // 2)
         own = xy.at[:, e, 0, c]
-        send(own, own, sib_send, sib_recv.at[e, 0], sib)
         if reach[0] > 0:
             send(own, xy.at[:, e, 1, c], ring_send, ring_recv.at[e, 1], along_y(-1))
         if reach[1] > 0:
@@ -121,6 +121,8 @@
         xy[1, e, 0, c] = dot(scaled_sel, og[...], (1, 0)).astype(BF16)
         if e == 0:
             pl.semaphore_wait(barrier, len(peers))
+        own = xy.at[:, e, 0, c]
+        send(own, own, sib_send, sib_recv.at[e, 0], sib)
         if e == 0:
             spread(0)
     loads[2].wait()
@@ -131,9 +133,11 @@
         return odd * ((i + 1) // 2) + (1 - odd) * ((ny - i // 2) % ny)
 
     def unit(u):
-        e = u // ny
-        i = u - e * ny
-        return e, far((i + e) % ny)
+        own = 1 - jnp.minimum(u // 2, 1)
+        late = jnp.minimum((u + own * ny) // (ny + 1), 1)
+        e = own * u + (1 - own) * late
+        i = (1 - own) * ((1 - late) * (u - 1) + late * (units - u))
+        return e, far(i)
 
     def pass_on(e, j):
         reach = (ny // 2, ny // 2 - 1) if e == 0 else (ny // 2 - 1, ny // 2)
@@ -184,10 +188,10 @@
                 + r2[u, half].astype(F32)
             )
             activated, slope = gelu_parts(total[0])
-            ad[e, 2 * h + q, 0, j, half] = activated.astype(BF16)
-            ad[e, 2 * h + q, 1, j, half] = (total[1] * slope).astype(BF16)
-            piece = ad.at[e, 2 * h + q, :, j, half]
-            send(piece, piece, a1_send, a1_recv.at[u], to)
+            act[e, 2 * h + q, j, half] = activated.astype(BF16)
+            dlt[e, 2 * h + q, j, half] = (total[1] * slope).astype(BF16)
+            piece = dlt.at[e, 2 * h + q, j, half]
+            send(piece, piece, d1_send, d1_recv.at[u], to)
             terms.append(activated * total[1])
         high, low = split(jnp.concatenate(terms, axis=0))
         ones = jnp.ones((16, 2 * 128), BF16)
@@ -196,16 +200,27 @@
 
     def widen(u):
         e, j = unit(u)
-        done(r2.at[u], a1_recv.at[u])
+        done(r2.at[u, 0], d1_recv.at[u])
         for half, (h, to) in enumerate(((h1, xa), (h2, xb))):
-            piece = ad.at[e, pl.ds(2 * h, 2), :, j, half]
-            send(piece, piece, a2_send, a2_recv.at[u], to)
+            piece = dlt.at[e, pl.ds(2 * h, 2), j, half]
+            send(piece, piece, d2_send, d2_recv.at[u], to)
+
+    def share_active(e):
+        for half, (h, q, to) in enumerate(((h1, q1, xb), (h2, q2, xa))):
+            piece = act.at[e, 2 * h + q, :, half]
+            send(piece, piece, a1_send, a1_recv.at[e], to)
+
+    def widen_active(e):
+        done(act.at[e, 0], a1_recv.at[e])
+        for half, (h, to) in enumerate(((h1, xa), (h2, xb))):
+            piece = act.at[e, pl.ds(2 * h, 2), :, half]
+            send(piece, piece, a2_send, a2_recv.at[e], to)
 
     def back(u):
         e, j = unit(u)
-        done(r1.at[u], a2_recv.at[u])
+        done(r2.at[u], d2_recv.at[u])
         delta = jnp.concatenate(
-            [ad[e, b, 1, j].reshape(2 * cap, 128) for b in range(4)], axis=1
+            [dlt[e, b, j].reshape(2 * cap, 128) for b in range(4)], axis=1
         )
         bk[u] = dot(delta, win[e], (1, 1)).astype(BF16).reshape(2, cap, -1)
         send(bk.at[u, 1 - c], pb.at[u], pb_send, pb_recv.at[u], sib)
@@ -224,21 +239,26 @@
             ys[u] = both
             send(ys.at[u], yr.at[e, j], y_send, y_recv.at[e, j], along_y(j))
 
-    def weight_grads(e, p):
-        rows = 2 * ny * cap
+    def two_blocks(ref, e, p):
+        return jnp.concatenate(
+            [ref[e, 2 * p + b].reshape(2 * ny * cap, 128) for b in range(2)], axis=1
+        )
+
+    def grad_in(e, p):
+        values = xy[0, e].reshape(2 * ny * cap, -1)
         cols = pl.ds(p * (hid // 2), hid // 2)
-        act, delta = (
-            jnp.concatenate([ad[e, 2 * p + b, a].reshape(rows, 128) for b in range(2)], axis=1)
-            for a in range(2)
-        )
-        gwi[e, :, cols] = dot(xy[0, e].reshape(rows, -1), delta, (0, 0)).astype(BF16)
-        gwo[e, cols, :] = dot(act, xy[1, e].reshape(rows, -1), (0, 0)).astype(BF16)
-
-    def store_grads(e):
-        return [
-            pltpu.make_async_copy(gwi.at[e], gwi_h.at[e], out_sem.at[e, 0]),
-            pltpu.make_async_copy(gwo.at[e], gwo_h.at[e], out_sem.at[e, 1]),
-        ]
+        gwi[e, :, cols] = dot(values, two_blocks(dlt, e, p), (0, 0)).astype(BF16)
+
+    def grad_out(e, p):
+        values = xy[1, e].reshape(2 * ny * cap, -1)
+        rows = pl.ds(p * (hid // 2), hid // 2)
+        gwo[e, rows, :] = dot(two_blocks(act, e, p), values, (0, 0)).astype(BF16)
+
+    def store_in(e):
+        return pltpu.make_async_copy(gwi.at[e], gwi_h.at[e], out_sem.at[e, 0])
+
+    def store_out(e):
+        return pltpu.make_async_copy(gwo.at[e], gwo_h.at[e], out_sem.at[e, 1])
 
     def step(k, carry):
         def stage(lag, work):
@@ -251,9 +271,9 @@
         stage(LAGS[2], widen)
         stage(0, products)
 
-        @pl.when(k < ny - 1)
-        def _():
-            pass_on(0, far(k + 1))
+        @pl.when((k > 0) & (k < ny))
+        def _():
+            pass_on(0, far(k))
 
         @pl.when(k == SECOND)
         def _():
@@ -285,19 +305,31 @@
             for d in range(1, ny):
                 send(gt.at[d], gy.at[d], gy_send, gy_recv, along_y(d))
 
+        @pl.when(k == units)
+        def _():
+            share_active(0)
+
+        @pl.when(k == units - 1 + LAGS[1])
+        def _():
+            share_active(1)
+
+        @pl.when(k == units - 1 + LAGS[2])
+        def _():
+            widen_active(0)
+
         for p in range(2):
-            @pl.when(k == ny + LAGS[3] + p)
+            @pl.when(k == ny + 1 + LAGS[3] + p)
             def _():
-                weight_grads(0, p)
-
-        @pl.when(k == ny + LAGS[3] + 2)
-        def _():
-            for copy in store_grads(0):
-                copy.start()
+                grad_in(0, p)
+
+        @pl.when(k == ny + 3 + LAGS[3])
+        def _():
+            store_in(0).start()
 
         return carry
 
     lax.fori_loop(0, units + LAGS[4], step, 0)
+    widen_active(1)
 
     rows = []
     for e in range(2):
@@ -329,9 +361,13 @@
         send(gz, gzr.at[d], gz_send, gz_recv, along_z(d))
 
     for p in range(2):
-        weight_grads(1, p)
-    for copy in store_grads(1):
-        copy.start()
+        grad_in(1, p)
+    store_in(1).start()
+    for e in range(2):
+        done(act.at[e, pl.ds(0, 2)], a2_recv.at[e])
+        for p in range(2):
+            grad_out(e, p)
+        store_out(e).start()
 
     out = tb[z].astype(F32)
     gates = gz[...]
@@ -356,8 +392,10 @@
     done(xy.at[:, :, :, 0], sib_send)
     done(r1, r1_send)
     done(r2, r2_send)
-    done(r2, a1_send)
-    done(r1, a2_send)
+    done(r2.at[:, 0], d1_send)
+    done(r2, d2_send)
+    done(act.at[:, 0], a1_send)
+    done(act.at[:, pl.ds(0, 2)], a2_send)
     done(pb, pb_send)
     done(ys.at[pl.ds(0, 2 * (ny - 1))], y_send)
     done(gx, gx_send)
@@ -367,8 +405,8 @@
         done(zr.at[pl.ds(1, nz - 1)], z_send)
         done(gzr.at[pl.ds(1, nz - 1)], gz_send)
     for e in range(2):
-        for copy in store_grads(e):
-            copy.wait()
+        store_in(e).wait()
+        store_out(e).wait()
 
 
 def hand_over(*refs):
@@ -414,7 +452,8 @@
             buf((units, 2, 2, 2, cap, 128), BF16),
             buf((units, 2, 2, cap, 128), BF16),
             buf((units, 2, 2, cap, 128), BF16),
-            buf((2, 4, 2, ny, 2, cap, 128), BF16),
+            buf((2, 4, ny, 2, cap, 128), BF16),
+            buf((2, 4, ny, 2, cap, 128), BF16),
             buf((units, 2, cap, width), BF16),
             buf((units, cap, width), BF16),
             buf((units, cap, width), BF16),
@@ -445,6 +484,10 @@
             dma((units,)),
             dma,
             dma((units,)),
+            dma,
+            dma((2,)),
+            dma,
+            dma((2,)),
             dma,
             dma((units,)),
             dma,

time: 98.3 us -> 92.8 us (0.944)
  Pallas kernels: 97.1 us -> 92 us
    pallas_call x1, Pallas kernels: 94.5 us -> 89.3 us  [body(): pl.pallas_call(functools.partial(kernel, ny, nz), out_shape=(jax.ShapeDty...]
where the time goes in v3:
time: 92.8 us; the launch traced here: 92.6 us
  Pallas kernels  92 us (99%)
    pallas_call x1, Pallas kernels, body(): pl.pallas_call(functools.partial(kernel, ny, nz), out_shape=(jax.ShapeDty...  89.3 us
    pallas_call x1, Pallas kernels, body(): pl.pallas_call(hand_over, out_shape=tuple((jax.ShapeDtypeStruct(r.shape,...  2.63 us

profile of v3, /device:TPU:1, one launch (start us, length us, event | category | flops | bytes accessed | tf_op | source)
XLA Modules:
  0.0 92.6 jit_solution(16227648163106661971)
XLA Ops:
  0.6 89.3 %expert_backward.1 = (bf16[32,512]{1,0:T(8,128)(2,1)}, f32[2,32]{1,0:T(2,128)}, bf16[2,512,512]{2,1,0:T(8,128)(2,1)}, bf16[2,512,512]{2,1,0:T(8,128)(2,1)}) custom-call(s32[2,256]{1,0:T(2,128)} %bitcast.3, bf16[2,256]{1,0:T(2,128)(2,1)} %bitcast.4, bf16[256,512]{1,0:T(8,128)(2,1)} %tok_h.1, bf16[256,512]{1,0:T(8,128)(2,1)} %og_h.1, ...), custom_call_target="tpu_custom_call" | custom-call | tf_op jit(solution)/shard_map/expert_backward/pallas_call | solution.py:434
  90.0 2.6 %hand_over.1 = (bf16[32,512]{1,0:T(8,128)(2,1)}, f32[2,32]{1,0:T(2,128)}, bf16[2,512,512]{2,1,0:T(8,128)(2,1)}, bf16[2,512,512]{2,1,0:T(8,128)(2,1)}) custom-call(bf16[32,512]{1,0:T(8,128)(2,1)} %get-tuple-element.12.refs_0_, f32[2,32]{1,0:T(2,128)} %get-tuple-element.13.refs_1_, bf16[2,512,512]{2,1,0:T(8,128)(2,1)} %get-tuple-element.14.refs_2_, ...), custom_call_target="tpu_custom_call" | custom-call | tf_op jit(solution)/shard_map/hand_over/pallas_call | solution.py:511

commit v4 on v3

--- a/solution.py
+++ b/solution.py
@@ -13,7 +13,7 @@
 gelu_cubic = 0.044715
 VMEM_BYTES = 62 * 2**20
 LAGS = (2, 4, 6, 8, 9)
-SECOND = 1
+SECOND = 4
 
 
 def gelu_parts(pre_act):
@@ -136,8 +136,10 @@
         own = 1 - jnp.minimum(u // 2, 1)
         late = jnp.minimum((u + own * ny) // (ny + 1), 1)
         e = own * u + (1 - own) * late
-        i = (1 - own) * ((1 - late) * (u - 1) + late * (units - u))
-        return e, far(i)
+        v = u - ny - 1
+        last = jnp.minimum((v + 3) // ny, 1) * late
+        second = (1 - last) * (v + 3) + last * (ny - 1 - v)
+        return e, far((1 - own) * ((1 - late) * (u - 1) + late * second))
 
     def pass_on(e, j):
         reach = (ny // 2, ny // 2 - 1) if e == 0 else (ny // 2 - 1, ny // 2)
@@ -266,10 +268,10 @@
             def _():
                 work(k - lag)
 
+        stage(0, products)
         stage(LAGS[0], halve)
         stage(LAGS[1], activate)
         stage(LAGS[2], widen)
-        stage(0, products)
 
         @pl.when((k > 0) & (k < ny))
         def _():
@@ -305,17 +307,13 @@
             for d in range(1, ny):
                 send(gt.at[d], gy.at[d], gy_send, gy_recv, along_y(d))
 
-        @pl.when(k == units)
+        @pl.when(k == units - 1 + LAGS[1])
         def _():
             share_active(0)
 
-        @pl.when(k == units - 1 + LAGS[1])
+        @pl.when(k == units - 1 + LAGS[2])
         def _():
             share_active(1)
-
-        @pl.when(k == units - 1 + LAGS[2])
-        def _():
-            widen_active(0)
 
         for p in range(2):
             @pl.when(k == ny + 1 + LAGS[3] + p)
@@ -329,6 +327,7 @@
         return carry
 
     lax.fori_loop(0, units + LAGS[4], step, 0)
+    widen_active(0)
     widen_active(1)
 
     rows = []
@@ -363,12 +362,14 @@
     for p in range(2):
         grad_in(1, p)
     store_in(1).start()
-    for e in range(2):
+
+    def finish_out(e):
         done(act.at[e, pl.ds(0, 2)], a2_recv.at[e])
         for p in range(2):
             grad_out(e, p)
         store_out(e).start()
 
+    finish_out(0)
     out = tb[z].astype(F32)
     gates = gz[...]
     if nz > 1:
@@ -387,6 +388,8 @@
     ).astype(BF16)
     high, low = split(jnp.concatenate((gates, jnp.zeros_like(gates)), axis=0))
     ggate[...] = (dot(high, pick, (1, 1)) + dot(low, pick, (1, 1)))[0:2, :]
+
+    finish_out(1)
 
     done(xy.at[:, :, pl.ds(0, ny - 1), 0], ring_send)
     done(xy.at[:, :, :, 0], sib_send)

time: 92.8 us -> 90.7 us (0.977)
  Pallas kernels: 92 us -> 89.9 us
    pallas_call x1, Pallas kernels: 89.3 us -> 87.2 us  [body(): pl.pallas_call(functools.partial(kernel, ny, nz), out_shape=(jax.ShapeDty...]
where the time goes in v4:
time: 90.7 us; the launch traced here: 90.5 us
  Pallas kernels  89.9 us (99%)
    pallas_call x1, Pallas kernels, body(): pl.pallas_call(functools.partial(kernel, ny, nz), out_shape=(jax.ShapeDty...  87.2 us
    pallas_call x1, Pallas kernels, body(): pl.pallas_call(hand_over, out_shape=tuple((jax.ShapeDtypeStruct(r.shape,...  2.63 us

profile of v4, /device:TPU:1, one launch (start us, length us, event | category | flops | bytes accessed | tf_op | source)
XLA Modules:
  0.0 90.5 jit_solution(2586264207722462280)
XLA Ops:
  0.6 87.2 %expert_backward.1 = (bf16[32,512]{1,0:T(8,128)(2,1)}, f32[2,32]{1,0:T(2,128)}, bf16[2,512,512]{2,1,0:T(8,128)(2,1)}, bf16[2,512,512]{2,1,0:T(8,128)(2,1)}) custom-call(s32[2,256]{1,0:T(2,128)} %bitcast.3, bf16[2,256]{1,0:T(2,128)(2,1)} %bitcast.4, bf16[256,512]{1,0:T(8,128)(2,1)} %tok_h.1, bf16[256,512]{1,0:T(8,128)(2,1)} %og_h.1, ...), custom_call_target="tpu_custom_call" | custom-call | tf_op jit(solution)/shard_map/expert_backward/pallas_call | solution.py:437
  87.9 2.6 %hand_over.1 = (bf16[32,512]{1,0:T(8,128)(2,1)}, f32[2,32]{1,0:T(2,128)}, bf16[2,512,512]{2,1,0:T(8,128)(2,1)}, bf16[2,512,512]{2,1,0:T(8,128)(2,1)}) custom-call(bf16[32,512]{1,0:T(8,128)(2,1)} %get-tuple-element.12.refs_0_, f32[2,32]{1,0:T(2,128)} %get-tuple-element.13.refs_1_, bf16[2,512,512]{2,1,0:T(8,128)(2,1)} %get-tuple-element.14.refs_2_, ...), custom_call_target="tpu_custom_call" | custom-call | tf_op jit(solution)/shard_map/hand_over/pallas_call | solution.py:514

commit v5 on v4

--- a/solution.py
+++ b/solution.py
@@ -339,7 +339,7 @@
         own = dot(sel[e], rows[e], (0, 0))
         total = own if e == 0 else total + own
     tb[...] = total.astype(BF16).reshape(tb.shape)
-    for d in range(1, nz):
+    for d in sorted(range(1, nz), key=lambda d: -min(d, nz - d)):
         send(tb.at[(z + d) % nz], zr.at[d], z_send, z_recv, along_z(d))
 
     done(gy.at[pl.ds(1, ny - 1)], gy_recv)
@@ -370,6 +370,7 @@
         store_out(e).start()
 
     finish_out(0)
+    finish_out(1)
     out = tb[z].astype(F32)
     gates = gz[...]
     if nz > 1:
@@ -388,8 +389,6 @@
     ).astype(BF16)
     high, low = split(jnp.concatenate((gates, jnp.zeros_like(gates)), axis=0))
     ggate[...] = (dot(high, pick, (1, 1)) + dot(low, pick, (1, 1)))[0:2, :]
-
-    finish_out(1)
 
     done(xy.at[:, :, pl.ds(0, ny - 1), 0], ring_send)
     done(xy.at[:, :, :, 0], sib_send)
@@ -414,8 +413,12 @@
 
 def hand_over(*refs):
     given, out, held, sems = refs[:4], refs[4:8], refs[8:12], refs[12]
-    loads = [pltpu.make_async_copy(given[i], held[i], sems.at[0, i]) for i in range(4)]
-    stores = [pltpu.make_async_copy(held[i], out[i], sems.at[1, i]) for i in range(4)]
+    pieces = [(2, 0), (3, 0), (2, 1), (3, 1), (0, None), (1, None)]
+    loads, stores = [], []
+    for n, (i, e) in enumerate(pieces):
+        a, b, d = (r[i] if e is None else r[i].at[e] for r in (given, held, out))
+        loads.append(pltpu.make_async_copy(a, b, sems.at[0, n]))
+        stores.append(pltpu.make_async_copy(b, d, sems.at[1, n]))
     for load in loads:
         load.start()
     for load, store in zip(loads, stores):
@@ -516,7 +519,7 @@
         out_shape=tuple(jax.ShapeDtypeStruct(r.shape, r.dtype) for r in results),
         in_specs=[anywhere] * 4,
         out_specs=(anywhere,) * 4,
-        scratch_shapes=[buf(r.shape, r.dtype) for r in results] + [dma((2, 4))],
+        scratch_shapes=[buf(r.shape, r.dtype) for r in results] + [dma((2, 6))],
         compiler_params=pltpu.CompilerParams(vmem_limit_bytes=VMEM_BYTES),
         name="hand_over",
     )(*results)

time: 90.7 us -> 89.1 us (0.982)
  Pallas kernels: 89.9 us -> 88.3 us
    pallas_call x1, Pallas kernels: 87.2 us -> 85.8 us  [body(): pl.pallas_call(functools.partial(kernel, ny, nz), out_shape=(jax.ShapeDty...]
where the time goes in v5:
time: 89.1 us; the launch traced here: 88.9 us
  Pallas kernels  88.3 us (99%)
    pallas_call x1, Pallas kernels, body(): pl.pallas_call(functools.partial(kernel, ny, nz), out_shape=(jax.ShapeDty...  85.8 us
    pallas_call x1, Pallas kernels, body(): pl.pallas_call(hand_over, out_shape=tuple((jax.ShapeDtypeStruct(r.shape,...  2.46 us

profile of v5, /device:TPU:1, one launch (start us, length us, event | category | flops | bytes accessed | tf_op | source)
XLA Modules:
  0.0 88.9 jit_solution(12851617752067129445)
XLA Ops:
  0.6 85.8 %expert_backward.1 = (bf16[32,512]{1,0:T(8,128)(2,1)}, f32[2,32]{1,0:T(2,128)}, bf16[2,512,512]{2,1,0:T(8,128)(2,1)}, bf16[2,512,512]{2,1,0:T(8,128)(2,1)}) custom-call(s32[2,256]{1,0:T(2,128)} %bitcast.3, bf16[2,256]{1,0:T(2,128)(2,1)} %bitcast.4, bf16[256,512]{1,0:T(8,128)(2,1)} %tok_h.1, bf16[256,512]{1,0:T(8,128)(2,1)} %og_h.1, ...), custom_call_target="tpu_custom_call" | custom-call | tf_op jit(solution)/shard_map/expert_backward/pallas_call | solution.py:440
  86.5 2.5 %hand_over.1 = (bf16[32,512]{1,0:T(8,128)(2,1)}, f32[2,32]{1,0:T(2,128)}, bf16[2,512,512]{2,1,0:T(8,128)(2,1)}, bf16[2,512,512]{2,1,0:T(8,128)(2,1)}) custom-call(bf16[32,512]{1,0:T(8,128)(2,1)} %get-tuple-element.12.refs_0_, f32[2,32]{1,0:T(2,128)} %get-tuple-element.13.refs_1_, bf16[2,512,512]{2,1,0:T(8,128)(2,1)} %get-tuple-element.14.refs_2_, ...), custom_call_target="tpu_custom_call" | custom-call | tf_op jit(solution)/shard_map/hand_over/pallas_call | solution.py:517
